TPU v7x, 32 devices: a whole 2x2x4 slice. The times are simulated.
32 devices in a mesh: grp: 4 (over z), ep: 8 (over y, x, core).
Axes of the slice: x: 2, y: 2, z: 4, core: 2. Of those that a mesh axis runs over, the one named last changes fastest.
Arguments:
- tokens: bfloat16 [4096, 2048], P(('grp', 'ep')), may hold values from -6 to 6
- out_grad: bfloat16 [4096, 2048], P(('grp', 'ep')), may hold values from -1.5 to 1.5
- routes: int32 [4096, 2], P(('grp', 'ep')), may hold values from 0 to 3, as said below
- gates: bfloat16 [4096, 2], P(('grp', 'ep')), may hold values from 0.099609375 to 1
- w_gate_up: bfloat16 [8, 2048, 1024], P('ep', 'grp'), may hold values from -0.125 to 0.125
- w_down: bfloat16 [8, 2048, 512], P('ep', 'grp'), may hold values from -0.25 to 0.25
- plan: int32 [8], replicated, may hold values from 0 to 3, as said below
- failed: int32 [4, 8], replicated, may hold values from 0 to 1, as said below
Outputs:
- token_grad: bfloat16 [4096, 2048], P(('grp', 'ep'))
- gate_grad: bfloat16 [4096, 2], P(('grp', 'ep'))
- weight_grad: float32 [4, 2048, 1536], P(None, ('grp', 'ep'))
Inputs may be any that keep to these rules, and one draw needn't show every extreme that they name: `plan`: each expert is hosted by one or three slots. Each group has one to 1 failed slots, and every expert keeps a live replica in every group. A token names 2 different experts. Under the replica rule the routes of one device reach any slot at most 40 times, and in every group some slot receives exactly 40 routes from every device of the group.
All inputs are finite; a program needn't handle non-finite values.
Results may differ from a plain program's by a relative error of at most 0.0058.
Values may be sent and summed in bfloat16 or wider, within the bound.
A program may use at most 128 MiB of HBM per device.

v0:
```python
import jax
import jax.numpy as jnp
from jax import lax
from jax.sharding import PartitionSpec as P


def assign(route_ids, hosting, in_service, capacity, experts):
    route_count = route_ids.shape[0] * route_ids.shape[1]
    slot_count = hosting.shape[0]
    flat_routes = route_ids.reshape(route_count)
    expert_ids = jnp.arange(experts, dtype=jnp.int32)
    hosted = ((hosting[None, :] == expert_ids[:, None]) & (in_service[None, :] > 0)).astype(
        jnp.int32
    )
    replicas = jnp.sum(hosted, axis=1)
    ordinal = jnp.sum(hosted * (jnp.cumsum(hosted, axis=1) - 1), axis=0)
    expert_hot = (flat_routes[:, None] == expert_ids[None, :]).astype(jnp.int32)
    expert_rank = jnp.sum(expert_hot * (jnp.cumsum(expert_hot, axis=0) - 1), axis=1)
    route_replicas = jnp.sum(expert_hot * replicas[None, :], axis=1)
    replica_pick = expert_rank % route_replicas
    slot_hot = (
        (hosting[None, :] == flat_routes[:, None])
        & (in_service[None, :] > 0)
        & (ordinal[None, :] == replica_pick[:, None])
    ).astype(jnp.int32)
    slot_rank = jnp.sum(slot_hot * (jnp.cumsum(slot_hot, axis=0) - 1), axis=1)
    slot_index = jnp.sum(slot_hot * jnp.arange(slot_count, dtype=jnp.int32)[None, :], axis=1)
    return slot_index * capacity + slot_rank


def expert_rows(rows_x, rows_dy, rows_gate, full_gu, full_dn):
    hidden_width = full_dn.shape[1]
    projected = jnp.dot(rows_x, full_gu, preferred_element_type=jnp.float32)
    gate_pre = projected[:, :hidden_width]
    up_pre = projected[:, hidden_width:]
    sigmoid_a = jax.nn.sigmoid(gate_pre)
    silu_a = gate_pre * sigmoid_a
    hidden = (silu_a * up_pre).astype(jnp.bfloat16)
    upstream = jnp.dot(rows_dy, full_dn, preferred_element_type=jnp.float32)
    rebuilt = lax.dot_general(
        hidden, full_dn, (((1,), (1,)), ((), ())), preferred_element_type=jnp.float32
    )
    gate_grad = jnp.sum(rows_dy.astype(jnp.float32) * rebuilt, axis=1).astype(jnp.bfloat16)
    gate_value = rows_gate.astype(jnp.float32)[:, None]
    hidden_grad = gate_value * upstream
    gate_delta = hidden_grad * up_pre * sigmoid_a * (1.0 + gate_pre * (1.0 - sigmoid_a))
    up_delta = hidden_grad * silu_a
    pre_grad = jnp.concatenate([gate_delta, up_delta], axis=1).astype(jnp.bfloat16)
    row_grad = lax.dot_general(
        pre_grad, full_gu, (((1,), (1,)), ((), ())), preferred_element_type=jnp.float32
    ).astype(jnp.bfloat16)
    gated_hidden = (gate_value * hidden.astype(jnp.float32)).astype(jnp.bfloat16)
    grad_gu = lax.dot_general(
        rows_x, pre_grad, (((0,), (0,)), ((), ())), preferred_element_type=jnp.float32
    )
    grad_dn = lax.dot_general(
        rows_dy, gated_hidden, (((0,), (0,)), ((), ())), preferred_element_type=jnp.float32
    )
    return (row_grad, gate_grad, grad_gu, grad_dn)


def local(tokens, out_grad, routes, gates, w_gate_up, w_down, plan, failed):
    groups = lax.axis_size("grp")
    slot_count = lax.axis_size("ep")
    my_group = lax.axis_index("grp")
    tok_count, model_width = tokens.shape
    topk_count = routes.shape[1]
    experts = slot_count // 2
    capacity = tok_count * topk_count * 5 // (4 * slot_count)
    route_count = tok_count * topk_count
    buffer_rows = slot_count * capacity
    in_service = 1 - lax.dynamic_index_in_dim(failed, my_group, 0, keepdims=False)
    positions = assign(routes, plan, in_service, capacity, experts)
    source = (
        jnp.full((buffer_rows,), route_count, jnp.int32)
        .at[positions]
        .set(jnp.arange(route_count, dtype=jnp.int32))
    )
    token_of = source // topk_count
    zero_row = jnp.zeros((1, model_width), jnp.bfloat16)
    send_x = jnp.concatenate([tokens, zero_row], axis=0)[token_of].reshape(
        slot_count, capacity, model_width
    )
    send_dy = jnp.concatenate([out_grad, zero_row], axis=0)[token_of].reshape(
        slot_count, capacity, model_width
    )
    send_gate = jnp.concatenate([gates.reshape(route_count), jnp.zeros((1,), jnp.bfloat16)])[source]
    send_gate = send_gate.reshape(slot_count, capacity)
    recv_x, recv_dy, recv_gate = (
        lax.all_to_all(send_x, "ep", split_axis=0, concat_axis=0, tiled=True),
        lax.all_to_all(send_dy, "ep", split_axis=0, concat_axis=0, tiled=True),
        lax.all_to_all(send_gate, "ep", split_axis=0, concat_axis=0, tiled=True),
    )
    full_gu, full_dn = (
        lax.all_gather(w_gate_up, "grp", axis=1, tiled=True),
        lax.all_gather(w_down, "grp", axis=1, tiled=True),
    )
    full_gu = full_gu[0]
    full_dn = full_dn[0]
    hidden_width = full_dn.shape[1]
    flat_x = recv_x.reshape(buffer_rows, model_width)
    flat_dy = recv_dy.reshape(buffer_rows, model_width)
    flat_gate = recv_gate.reshape(buffer_rows)
    row_grads, gate_rows, grad_gu, grad_dn = expert_rows(
        flat_x, flat_dy, flat_gate, full_gu, full_dn
    )
    back_x, back_gate = (
        lax.all_to_all(
            row_grads.reshape(slot_count, capacity, model_width),
            "ep",
            split_axis=0,
            concat_axis=0,
            tiled=True,
        ),
        lax.all_to_all(
            gate_rows.reshape(slot_count, capacity), "ep", split_axis=0, concat_axis=0, tiled=True
        ),
    )
    route_rows = back_x.reshape(buffer_rows, model_width)[positions]
    token_grad = jnp.sum(
        route_rows.reshape(tok_count, topk_count, model_width).astype(jnp.float32), axis=1
    ).astype(jnp.bfloat16)
    gate_grad = back_gate.reshape(buffer_rows)[positions].reshape(tok_count, topk_count)
    columns = 3 * hidden_width
    rows_each = model_width // (groups * slot_count)
    slot_grad = jnp.concatenate([grad_gu, grad_dn], axis=1).astype(jnp.bfloat16)
    slot_grad = slot_grad.reshape(groups, slot_count, rows_each, columns)
    expert_ids = jnp.arange(experts, dtype=jnp.int32)
    mixed = lax.all_to_all(
        lax.all_to_all(slot_grad, "grp", split_axis=0, concat_axis=0, tiled=True),
        "ep",
        split_axis=1,
        concat_axis=1,
        tiled=True,
    )
    hosted_all = (
        (plan[None, None, :] == expert_ids[None, :, None]) & (failed[:, None, :] == 0)
    ).astype(jnp.bfloat16)
    per_group = jnp.einsum("ges,gsrc->gerc", hosted_all, mixed, preferred_element_type=jnp.float32)
    weight_grad = jnp.sum(per_group, axis=0) / groups
    return (token_grad, gate_grad, weight_grad)


def solution(mesh):
    placed = (
        P(("grp", "ep"), None),
        P(("grp", "ep"), None),
        P(("grp", "ep"), None),
        P(("grp", "ep"), None),
        P("ep", "grp", None),
        P("ep", "grp", None),
        P(),
        P(),
    )
    return jax.shard_map(
        local,
        mesh=mesh,
        in_specs=placed,
        out_specs=(P(("grp", "ep"), None), P(("grp", "ep"), None), P(None, ("grp", "ep"), None)),
        check_vma=False,
    )
```

profile of v0, /device:TPU:0, one launch (start us, length us, event | category | flops | bytes accessed | tf_op | source)
XLA Modules:
  0.0 418.6 jit_solution(2920890068866724111)
XLA Ops:
  17.4 5.2 %all-to-all-start = ((bf16[8,1,40]{2,1,0:T(2,128)(2,1)}), bf16[8,1,40]{2,1,0:T(2,128)(2,1)S(1)}, u32[]{:S(2)}, u32[]{:S(2)}) async-start(bf16[8,1,40]{2,1,0:T(2,128)(2,1)} %all_to_all.33), calls=%async_computation | async-start | bytes 8192 | tf_op jit(solution)/shard_map/all_to_all | solution.py:92
  22.6 3.0 gather_fusion.1
  27.1 3.6 all-to-all-start.1
  30.8 3.0 gather_fusion.2
  33.8 15.0 %all-to-all-done.1 = bf16[8,40,2048]{2,1,0:T(8,128)(2,1)S(1)} async-done(((bf16[8,40,2048]{2,1,0:T(8,128)(2,1)}), bf16[8,40,2048]{2,1,0:T(8,128)(2,1)S(1)}, u32[]{:S(2)}, u32[]{:S(2)}) %all-to-all-start.1) | async-done | bytes 1310752 | tf_op jit(solution)/shard_map/all_to_all | solution.py:91
  48.9 3.6 all-to-all-start.2
  54.1 16.5 %all-to-all-done.2 = bf16[8,40,2048]{2,1,0:T(8,128)(2,1)S(1)} async-done(((bf16[8,40,2048]{2,1,0:T(8,128)(2,1)}), bf16[8,40,2048]{2,1,0:T(8,128)(2,1)S(1)}, u32[]{:S(2)}, u32[]{:S(2)}) %all-to-all-start.2) | async-done | bytes 1310752 | tf_op jit(solution)/shard_map/all_to_all | solution.py:90
  72.1 21.0 %all-gather.5.cloned.1.call-done = bf16[1,2048,1024]{2,1,0:T(8,128)(2,1)} async-done(((bf16[1,512,1024]{2,1,0:T(8,128)(2,1)}), bf16[1,2048,1024]{2,1,0:T(8,128)(2,1)}) %all-gather.5.cloned.1.call-update) | async-done | bytes 4194320 | tf_op jit(solution)/shard_map/all_gather | solution.py:95
  93.2 4.8 %fusion.4 = f32[320,1024]{1,0:T(8,128)} fusion(bf16[320,2048]{1,0:T(8,128)(2,1)S(1)} %bitcast.81, bf16[1,2048,1024]{2,1,0:T(8,128)(2,1)} %all-gather.5.cloned.1.call-done), kind=kOutput, calls=%fused_computation.11 | convolution fusion | flops 1342177280 | bytes 6815744 | tf_op jit(solution)/shard_map/dot_general | solution.py:33
  97.9 41.3 %all-gather.3.cloned.1.call-done = bf16[1,2048,512]{2,1,0:T(8,128)(2,1)} async-done(((bf16[1,512,512]{2,1,0:T(8,128)(2,1)}), bf16[1,2048,512]{2,1,0:T(8,128)(2,1)}) %all-gather.3.cloned.1.call-update) | async-done | bytes 2097168 | tf_op jit(solution)/shard_map/all_gather | solution.py:96
  139.2 3.9 multiply_convert_fusion.3
  144.9 3.6 all-to-all-start.4
  150.1 4.5 %convolution_convert_fusion = bf16[4,8,64,1024]{3,1,0,2:T(8,128)(2,1)} fusion(bf16[4,8,64,320]{3,2,1,0:T(8,128)(2,1)S(1)} %bitcast.83, bf16[320,512]{1,0:T(8,128)(2,1)S(1)} %copy-done.11, bf16[320,512]{1,0:T(8,128)(2,1)S(1)} %copy-done.9), kind=kOutput, calls=%fused_computation.17 | convolution fusion | flops 1345585152 | bytes 6160384 | tf_op jit(solution)/shard_map/dot_general | solution.py:53
  157.6 3.1 copy.45
  160.7 5.4 %all-to-all-start.5 = ((bf16[4,8,64,1536]{3,1,2,0:T(8,128)(2,1)}), bf16[4,8,64,1536]{3,1,2,0:T(8,128)(2,1)}, u32[]{:S(2)}, u32[]{:S(2)}) async-start(bf16[4,8,64,1536]{3,1,2,0:T(8,128)(2,1)} %copy.45), calls=%async_computation.5 | async-start | bytes 12582912 | tf_op jit(solution)/shard_map/all_to_all | solution.py:130
  166.1 4.8 %fusion.12 = bf16[320,2048]{1,0:T(8,128)(2,1)} fusion(bf16[1,2048,1024]{2,1,0:T(8,128)(2,1)} %all-gather.5.cloned.1.call-done, bf16[320,512]{1,0:T(8,128)(2,1)S(1)} %copy-done.12, bf16[320,512]{1,0:T(8,128)(2,1)S(1)} %copy-done.10), kind=kOutput, calls=%fused_computation.16 | convolution fusion | flops 1344143360 | bytes 6160384 | tf_op jit(solution)/shard_map/dot_general | solution.py:49
  170.9 134.3 %all-to-all-done.5 = bf16[4,8,64,1536]{3,1,2,0:T(8,128)(2,1)} async-done(((bf16[4,8,64,1536]{3,1,2,0:T(8,128)(2,1)}), bf16[4,8,64,1536]{3,1,2,0:T(8,128)(2,1)}, u32[]{:S(2)}, u32[]{:S(2)}) %all-to-all-start.5) | async-done | bytes 6291488 | tf_op jit(solution)/shard_map/all_to_all | solution.py:130
  305.2 3.8 all-to-all-start.3
  309.0 10.3 %copy.46 = bf16[4,8,64,1536]{3,0,2,1:T(4,128)(2,1)} copy(bf16[4,8,64,1536]{3,1,2,0:T(8,128)(2,1)} %all-to-all-done.5) | data formatting | bytes 12582912 | tf_op jit(solution)/shard_map/all_to_all | solution.py:130
  319.3 7.9 %all-to-all-done.3 = bf16[8,40,2048]{2,1,0:T(8,128)(2,1)S(1)} async-done(((bf16[8,40,2048]{2,1,0:T(8,128)(2,1)}), bf16[8,40,2048]{2,1,0:T(8,128)(2,1)S(1)}, u32[]{:S(2)}, u32[]{:S(2)}) %all-to-all-start.3) | async-done | bytes 1310752 | tf_op jit(solution)/shard_map/all_to_all | solution.py:108
  327.2 5.0 %all-to-all-start.6 = ((bf16[4,8,64,1536]{3,0,2,1:T(4,128)(2,1)}), bf16[4,8,64,1536]{3,0,2,1:T(4,128)(2,1)}, u32[]{:S(2)}, u32[]{:S(2)}) async-start(bf16[4,8,64,1536]{3,0,2,1:T(4,128)(2,1)} %copy.46), calls=%async_computation.6 | async-start | bytes 12582912 | tf_op jit(solution)/shard_map/all_to_all | solution.py:129
  337.1 3.6 reduce_sum.91
  340.8 62.8 %all-to-all-done.6 = bf16[4,8,64,1536]{3,0,2,1:T(4,128)(2,1)} async-done(((bf16[4,8,64,1536]{3,0,2,1:T(4,128)(2,1)}), bf16[4,8,64,1536]{3,0,2,1:T(4,128)(2,1)}, u32[]{:S(2)}, u32[]{:S(2)}) %all-to-all-start.6) | async-done | bytes 6291488 | tf_op jit(solution)/shard_map/all_to_all | solution.py:129
  403.6 6.6 %fusion.9 = f32[4,64,1536]{2,0,1:T(4,128)S(1)} fusion(bf16[4,8,64,1536]{3,0,2,1:T(4,128)(2,1)} %all-to-all-done.6, pred[4,8]{1,0:T(4,128)(4,1)S(1)} %broadcast_compare_fusion, pred[4,8]{1,0:T(4,128)(4,1)S(1)} %get-tuple-element.26), kind=kOutput, calls=%fused_computation.15 | convolution fusion | flops 25559168 | bytes 7864384 | tf_op jit(solution)/shard_map/ges,gsrc->gerc/dot_general | solution.py:139
  (87 shorter events, 27.5 us)
Async XLA Ops:
  7.2 1.5 copy-start.6
  7.2 3.6 copy-start.5
  7.2 3.6 copy-start.4
  7.2 5.3 %copy-start.7 = (bf16[128,2]{0,1:T(2,128)(2,1)S(1)}, bf16[128,2]{0,1:T(2,128)(2,1)}, u32[]{:S(2)}) copy-start(bf16[128,2]{0,1:T(2,128)(2,1)} %param.11) | copy-start | bytes 1540
  7.2 15.3 %copy-start.2 = (bf16[128,2048]{1,0:T(8,128)(2,1)S(1)}, bf16[128,2048]{1,0:T(8,128)(2,1)}, u32[]{:S(2)}) copy-start(bf16[128,2048]{1,0:T(8,128)(2,1)} %param.9) | copy-start | bytes 1572868
  7.2 85.9 %all-gather.5.cloned.1.call-start = ((), (), s32[]{:S(2)}) async-start(), calls=%async_computation.8 | async-start | bytes 5242880 | tf_op jit(solution)/shard_map/all_gather | solution.py:95
  8.0 131.3 %all-gather.3.cloned.1.call-start = ((), (), s32[]{:S(2)}) async-start(), calls=%async_computation.7 | async-start | bytes 2621440 | tf_op jit(solution)/shard_map/all_gather | solution.py:96
  17.4 9.8 %all-to-all-start = ((bf16[8,1,40]{2,1,0:T(2,128)(2,1)}), bf16[8,1,40]{2,1,0:T(2,128)(2,1)S(1)}, u32[]{:S(2)}, u32[]{:S(2)}) async-start(bf16[8,1,40]{2,1,0:T(2,128)(2,1)} %all_to_all.33), calls=%async_computation | async-start | bytes 8192 | tf_op jit(solution)/shard_map/all_to_all | solution.py:92
  25.6 5.1 %copy-start.3 = (bf16[128,2048]{1,0:T(8,128)(2,1)S(1)}, bf16[128,2048]{1,0:T(8,128)(2,1)}, u32[]{:S(2)}) copy-start(bf16[128,2048]{1,0:T(8,128)(2,1)} %param.8) | copy-start | bytes 1572868
  27.1 21.7 %all-to-all-start.1 = ((bf16[8,40,2048]{2,1,0:T(8,128)(2,1)}), bf16[8,40,2048]{2,1,0:T(8,128)(2,1)S(1)}, u32[]{:S(2)}, u32[]{:S(2)}) async-start(bf16[8,40,2048]{2,1,0:T(8,128)(2,1)} %bitcast.9), calls=%async_computation.1 | async-start | bytes 2621440 | tf_op jit(solution)/shard_map/all_to_all | solution.py:91
  48.9 21.7 %all-to-all-start.2 = ((bf16[8,40,2048]{2,1,0:T(8,128)(2,1)}), bf16[8,40,2048]{2,1,0:T(8,128)(2,1)S(1)}, u32[]{:S(2)}, u32[]{:S(2)}) async-start(bf16[8,40,2048]{2,1,0:T(8,128)(2,1)} %bitcast.12), calls=%async_computation.2 | async-start | bytes 2621440 | tf_op jit(solution)/shard_map/all_to_all | solution.py:90
  139.2 3.9 copy-start.8
  143.2 5.3 %copy-start = (bf16[2048,320]{1,0:T(8,128)(2,1)S(1)}, bf16[2048,320]{1,0:T(8,128)(2,1)}, u32[]{:S(2)}) copy-start(bf16[2048,320]{1,0:T(8,128)(2,1)} %copy.43) | copy-start | bytes 3932164
  144.9 15.8 %all-to-all-start.4 = ((bf16[8,1,40]{2,1,0:T(2,128)(2,1)}), bf16[8,1,40]{2,1,0:T(2,128)(2,1)S(1)}, u32[]{:S(2)}, u32[]{:S(2)}) async-start(bf16[8,1,40]{2,1,0:T(2,128)(2,1)} %convert_element_type.71), calls=%async_computation.4 | async-start | bytes 8192 | tf_op jit(solution)/shard_map/all_to_all | solution.py:115
  148.5 1.5 copy-start.1
  148.6 1.5 copy-start.9
  148.6 1.5 copy-start.11
  160.7 5.4 %copy-start.10 = (bf16[320,512]{1,0:T(8,128)(2,1)S(1)}, bf16[320,512]{1,0:T(8,128)(2,1)}, u32[]{:S(2)}) copy-start(bf16[320,512]{1,0:T(8,128)(2,1)} %get-tuple-element.21) | copy-start | bytes 983044
  160.7 5.4 %copy-start.12 = (bf16[320,512]{1,0:T(8,128)(2,1)S(1)}, bf16[320,512]{1,0:T(8,128)(2,1)}, u32[]{:S(2)}) copy-start(bf16[320,512]{1,0:T(8,128)(2,1)} %get-tuple-element.22) | copy-start | bytes 983044
  160.7 144.5 %all-to-all-start.5 = ((bf16[4,8,64,1536]{3,1,2,0:T(8,128)(2,1)}), bf16[4,8,64,1536]{3,1,2,0:T(8,128)(2,1)}, u32[]{:S(2)}, u32[]{:S(2)}) async-start(bf16[4,8,64,1536]{3,1,2,0:T(8,128)(2,1)} %copy.45), calls=%async_computation.5 | async-start | bytes 12582912 | tf_op jit(solution)/shard_map/all_to_all | solution.py:130
  305.2 22.1 %all-to-all-start.3 = ((bf16[8,40,2048]{2,1,0:T(8,128)(2,1)}), bf16[8,40,2048]{2,1,0:T(8,128)(2,1)S(1)}, u32[]{:S(2)}, u32[]{:S(2)}) async-start(bf16[8,40,2048]{2,1,0:T(8,128)(2,1)} %bitcast.15), calls=%async_computation.3 | async-start | bytes 2621440 | tf_op jit(solution)/shard_map/all_to_all | solution.py:108
  327.2 76.3 %all-to-all-start.6 = ((bf16[4,8,64,1536]{3,0,2,1:T(4,128)(2,1)}), bf16[4,8,64,1536]{3,0,2,1:T(4,128)(2,1)}, u32[]{:S(2)}, u32[]{:S(2)}) async-start(bf16[4,8,64,1536]{3,0,2,1:T(4,128)(2,1)} %copy.46), calls=%async_computation.6 | async-start | bytes 12582912 | tf_op jit(solution)/shard_map/all_to_all | solution.py:129
Sparse Core Ops, SparseCore 0:
  9.6 83.4 all-gather.4
  94.7 44.4 all-gather.2
where the time goes:
time: 419 us
  waiting for transfers between devices  302 us (72%)
  local copies, waits for them, and re-layouts  35.8 us (9%)
  starting transfers between devices  30.2 us (7%)
  matrix products  27 us (6%)
  between operations  14.4 us (3%)
  other arithmetic  9.48 us (2%)
    all_to_all x1, waiting for transfers between devices, local(): lax.all_to_all(slot_grad, 'grp', split_axis=0, concat_axis=0, tiled=True)  134 us
    all_to_all x1, waiting for transfers between devices, local(): lax.all_to_all(lax.all_to_all(slot_grad, 'grp', split_axis=0, concat_axis...  62.8 us
    all_gather x1, waiting for transfers between devices, local(): lax.all_gather(w_down, 'grp', axis=1, tiled=True)  41.3 us
    all_gather x1, waiting for transfers between devices, local(): lax.all_gather(w_gate_up, 'grp', axis=1, tiled=True)  21 us
    all_to_all x1, waiting for transfers between devices, local(): lax.all_to_all(send_x, 'ep', split_axis=0, concat_axis=0, tiled=True)  16.5 us
    all_to_all x1, waiting for transfers between devices, local(): lax.all_to_all(send_dy, 'ep', split_axis=0, concat_axis=0, tiled=True)  15 us
    all_to_all x1, local copies, waits for them, and re-layouts, local(): lax.all_to_all(slot_grad, 'grp', split_axis=0, concat_axis=0, tiled=True)  10.3 us
  transfers between devices with their start and end apart: 9, of which 8 were waited for; matrix products, arithmetic and copies ran while one was open for 14% of the time, Pallas kernels for 0%

commit v1 on v0

--- a/solution.py
+++ b/solution.py
@@ -1,6 +1,10 @@
+import functools
+
 import jax
 import jax.numpy as jnp
 from jax import lax
+from jax.experimental import pallas as pl
+from jax.experimental.pallas import tpu as pltpu
 from jax.sharding import PartitionSpec as P
 
 
@@ -25,7 +29,7 @@
     ).astype(jnp.int32)
     slot_rank = jnp.sum(slot_hot * (jnp.cumsum(slot_hot, axis=0) - 1), axis=1)
     slot_index = jnp.sum(slot_hot * jnp.arange(slot_count, dtype=jnp.int32)[None, :], axis=1)
-    return slot_index * capacity + slot_rank
+    return slot_index, slot_rank
 
 
 def expert_rows(rows_x, rows_dy, rows_gate, full_gu, full_dn):
@@ -59,6 +63,415 @@
     return (row_grad, gate_grad, grad_gu, grad_dn)
 
 
+MESH = pl.DeviceIdType.MESH
+LANES = 128
+ROW_TILE = 16
+
+
+def fused_kernel(
+    nz, ne, block,
+    tok_ref, dy_ref, pack_ref, unpack_ref, gate_ref, gu_ref, dn_ref, mask_ref,
+    tgrad_ref, ggrad_ref, wgrad_ref,
+    weights, send_rows, rows, x_t, dy_t, row_acc, gate_acc, slot_grads, peer_grads,
+    plane_sums, far_sums, ret, back,
+    ag_send, ag_recv, out_send, out_recv, grad_send, grad_recv, sum_send, sum_recv,
+    ret_send, ret_recv,
+):
+    z = lax.axis_index("grp")
+    me = lax.axis_index("ep")
+    chunks, _, shard, width3 = weights.shape
+    model = nz * shard
+    width = width3 // 3
+    hidden_width = chunks * width
+    experts = wgrad_ref.shape[0]
+    own_rows = wgrad_ref.shape[1]
+    count = ne * block
+    f32, bf16 = jnp.float32, jnp.bfloat16
+
+    barrier = pltpu.get_barrier_semaphore()
+    for k in range(1, ne):
+        pl.semaphore_signal(
+            barrier, inc=1, device_id={"ep": lax.rem(me + k, ne)}, device_id_type=MESH
+        )
+    for k in range(1, nz):
+        pl.semaphore_signal(
+            barrier, inc=1, device_id={"grp": lax.rem(z + k, nz)}, device_id_type=MESH
+        )
+
+    for f in range(chunks):
+        cols = slice(f * width, (f + 1) * width)
+        weights[f, z, :, 0:width] = gu_ref[0, :, cols]
+        weights[f, z, :, width : 2 * width] = gu_ref[
+            0, :, hidden_width + f * width : hidden_width + (f + 1) * width
+        ]
+        weights[f, z, :, 2 * width : 3 * width] = dn_ref[0, :, cols]
+    pl.semaphore_wait(barrier, ne - 1 + nz - 1)
+
+    def shard_copy(f, owner, up):
+        step = 1 if up else nz - 1
+        return pltpu.make_async_remote_copy(
+            src_ref=weights.at[f, owner],
+            dst_ref=weights.at[f, owner],
+            send_sem=ag_send.at[f, owner, 0 if up else 1],
+            recv_sem=ag_recv.at[f, owner],
+            device_id={"grp": lax.rem(z + step, nz)},
+            device_id_type=MESH,
+        )
+
+    def start_own(f):
+        @pl.when(z < nz - 1)
+        def _():
+            shard_copy(f, z, True).start()
+
+        @pl.when(z > 0)
+        def _():
+            shard_copy(f, z, False).start()
+
+    def arrive(f, hop):
+        @pl.when(z >= hop)
+        def _():
+            shard_copy(f, z - hop, True).wait_recv()
+
+            @pl.when(z < nz - 1)
+            def _():
+                shard_copy(f, z - hop, True).start()
+
+        @pl.when(z + hop < nz)
+        def _():
+            shard_copy(f, z + hop, False).wait_recv()
+
+            @pl.when(z > 0)
+            def _():
+                shard_copy(f, z + hop, False).start()
+
+    def shard_sends_done():
+        for f in range(chunks):
+            for hop in range(nz):
+                @pl.when((z >= hop) & (z < nz - 1))
+                def _():
+                    shard_copy(f, z - hop, True).wait_send()
+
+                @pl.when((z + hop < nz) & (z > 0))
+                def _():
+                    shard_copy(f, z + hop, False).wait_send()
+
+    def block_rows(k):
+        return pl.ds(pl.multiple_of(k * block, ROW_TILE), block)
+
+    def out_copy(k):
+        return pltpu.make_async_remote_copy(
+            src_ref=send_rows.at[block_rows(k)],
+            dst_ref=rows.at[block_rows(k)],
+            send_sem=out_send.at[k],
+            recv_sem=out_recv.at[k],
+            device_id={"ep": lax.rem(me + k, ne)},
+            device_id_type=MESH,
+        )
+
+    def pack(k, target):
+        here = block_rows(k)
+        first, second = pack_ref[0, here, :], pack_ref[1, here, :]
+        both = first + second
+        target[here, 0:model] = jnp.dot(
+            both, tok_ref[...], preferred_element_type=f32
+        ).astype(bf16)
+        target[here, model : 2 * model] = jnp.dot(
+            both, dy_ref[...], preferred_element_type=f32
+        ).astype(bf16)
+        target[here, 2 * model : 2 * model + LANES] = (
+            jnp.dot(first, gate_ref[0], preferred_element_type=f32)
+            + jnp.dot(second, gate_ref[1], preferred_element_type=f32)
+        ).astype(bf16)
+
+    def grad_copy(f, k):
+        return pltpu.make_async_remote_copy(
+            src_ref=slot_grads.at[f, lax.rem(me + k, ne)],
+            dst_ref=peer_grads.at[f, k],
+            send_sem=grad_send.at[f, k],
+            recv_sem=grad_recv.at[f, k],
+            device_id={"ep": lax.rem(me + k, ne)},
+            device_id_type=MESH,
+        )
+
+    def sum_copy(f, k):
+        return pltpu.make_async_remote_copy(
+            src_ref=plane_sums.at[f, lax.rem(z + k, nz)],
+            dst_ref=far_sums.at[f, k],
+            send_sem=sum_send.at[f, k],
+            recv_sem=sum_recv.at[f, k],
+            device_id={"grp": lax.rem(z + k, nz)},
+            device_id_type=MESH,
+        )
+
+    def ret_copy(k):
+        return pltpu.make_async_remote_copy(
+            src_ref=ret.at[block_rows(k)],
+            dst_ref=back.at[block_rows(k)],
+            send_sem=ret_send.at[k],
+            recv_sem=ret_recv.at[k],
+            device_id={"ep": lax.rem(me + ne - k, ne)},
+            device_id_type=MESH,
+        )
+
+    def compute(f):
+        x = rows[:, 0:model]
+        dy = rows[:, model : 2 * model]
+        gate = rows[:, 2 * model : 2 * model + LANES].astype(f32)
+        full = weights[f].reshape(model, width3)
+        pre = jnp.dot(x, full[:, 0 : 2 * width], preferred_element_type=f32)
+        upstream = jnp.dot(dy, full[:, 2 * width :], preferred_element_type=f32)
+        a, b = pre[:, :width], pre[:, width:]
+        sig = jax.nn.sigmoid(a)
+        silu = a * sig
+        hidden = (silu * b).astype(bf16)
+        hidden_f = hidden.astype(f32)
+        gate_part = upstream * hidden_f
+        if f == 0:
+            gate_acc[...] = gate_part
+        else:
+            gate_acc[...] += gate_part
+        hidden_grad = gate * upstream
+        da = hidden_grad * b * sig * (1.0 + a * (1.0 - sig))
+        db = hidden_grad * silu
+        pre_grad = jnp.concatenate([da, db], axis=1).astype(bf16)
+        gated = (gate * hidden_f).astype(bf16)
+
+        @pl.loop(0, nz)
+        def _(g):
+            here = pl.ds(pl.multiple_of(g * shard, shard), shard)
+            gu = jnp.dot(x_t[here, :], pre_grad, preferred_element_type=f32).astype(bf16)
+            dn = jnp.dot(dy_t[here, :], gated, preferred_element_type=f32).astype(bf16)
+            slot_grads[f, :, g, :, 0 : 2 * width] = gu.reshape(ne, own_rows, 2 * width)
+            slot_grads[f, :, g, :, 2 * width :] = dn.reshape(ne, own_rows, width)
+
+        for k in range(1, ne):
+            grad_copy(f, k).start()
+
+        @pl.loop(0, nz)
+        def _(g):
+            here = pl.ds(pl.multiple_of(g * shard, shard), shard)
+            part = lax.dot_general(
+                pre_grad,
+                weights[f, g, :, 0 : 2 * width],
+                (((1,), (1,)), ((), ())),
+                preferred_element_type=f32,
+            )
+            if f == 0:
+                row_acc[:, here] = part
+            elif f < chunks - 1:
+                row_acc[:, here] += part
+            else:
+                ret[:, here] = (row_acc[:, here] + part).astype(bf16)
+
+    def plane_sum(f):
+        for k in range(1, ne):
+            grad_copy(f, k).wait_recv()
+
+        @pl.loop(0, nz)
+        def _(g):
+            @pl.loop(0, own_rows // ROW_TILE)
+            def _(r):
+                here = pl.ds(pl.multiple_of(r * ROW_TILE, ROW_TILE), ROW_TILE)
+                total = [None] * experts
+                for k in range(ne):
+                    if k == 0:
+                        value = slot_grads[f, me, g, here, :].astype(f32)
+                    else:
+                        value = peer_grads[f, k, g, here, :].astype(f32)
+                    for e in range(experts):
+                        term = value * mask_ref[e, k]
+                        total[e] = term if total[e] is None else total[e] + term
+                for e in range(experts):
+                    plane_sums[f, g, e, here, :] = total[e].astype(bf16)
+
+        for k in range(1, nz):
+            sum_copy(f, k).start()
+
+    def finish(f):
+        for k in range(1, nz):
+            sum_copy(f, k).wait_recv()
+
+        @pl.loop(0, experts)
+        def _(e):
+            total = plane_sums[f, z, e].astype(f32)
+            for k in range(1, nz):
+                total = total + far_sums[f, k, e].astype(f32)
+            total = total / nz
+            for part in range(3):
+                start = part * hidden_width + f * width
+                wgrad_ref[e, :, start : start + width] = total[
+                    :, part * width : (part + 1) * width
+                ]
+
+    start_own(0)
+    if chunks > 1:
+        start_own(1)
+
+    @pl.loop(1, ne)
+    def _(k):
+        pack(k, send_rows)
+        out_copy(k).start()
+
+    pack(0, rows)
+
+    def rows_ready():
+        for k in range(1, ne):
+            out_copy(k).wait_recv()
+
+        @pl.loop(0, model // LANES)
+        def _(c):
+            here = pl.ds(pl.multiple_of(c * LANES, LANES), LANES)
+            there = pl.ds(pl.multiple_of(model + c * LANES, LANES), LANES)
+            x_t[here, :] = rows[:, here].T
+            dy_t[here, :] = rows[:, there].T
+
+    def hop_range(f, low, high):
+        for hop in range(low, min(high, nz)):
+            arrive(f, hop)
+
+    late = chunks > 1 and nz > 2
+    hop_range(0, 1, nz)
+    if not late:
+        rows_ready()
+        compute(0)
+    for f in range(1, chunks):
+        if f + 1 < chunks:
+            start_own(f + 1)
+        if f == 1 and late:
+            hop_range(1, 1, nz - 1)
+            rows_ready()
+            compute(0)
+            hop_range(1, nz - 1, nz)
+        else:
+            hop_range(f, 1, nz - 1)
+            if f >= 2:
+                plane_sum(f - 2)
+            hop_range(f, nz - 1, nz)
+        compute(f)
+
+    ret[:, model : model + LANES] = jnp.broadcast_to(
+        jnp.sum(gate_acc[...], axis=1, keepdims=True), (count, LANES)
+    ).astype(bf16)
+    for k in range(1, ne):
+        ret_copy(k).start()
+    back[0:block, :] = ret[0:block, :]
+    if chunks > 1:
+        plane_sum(chunks - 2)
+    for f in range(chunks - 2):
+        finish(f)
+    plane_sum(chunks - 1)
+
+    for k in range(1, ne):
+        ret_copy(k).wait_recv()
+    first, second = unpack_ref[0], unpack_ref[1]
+    both = first + second
+
+    @pl.loop(0, nz)
+    def _(g):
+        here = pl.ds(pl.multiple_of(g * shard, shard), shard)
+        tgrad_ref[:, here] = jnp.dot(
+            both, back[:, here], preferred_element_type=f32
+        ).astype(bf16)
+
+    gates_back = back[:, model : model + LANES]
+    lane = lax.broadcasted_iota(jnp.int32, ggrad_ref.shape, 1)
+    ggrad_ref[...] = jnp.where(
+        lane == 0,
+        jnp.dot(first, gates_back, preferred_element_type=f32),
+        jnp.dot(second, gates_back, preferred_element_type=f32),
+    ).astype(bf16)
+
+    for f in range(max(chunks - 2, 0), chunks):
+        finish(f)
+
+    shard_sends_done()
+    for k in range(1, ne):
+        out_copy(k).wait_send()
+        ret_copy(k).wait_send()
+    for f in range(chunks):
+        for k in range(1, ne):
+            grad_copy(f, k).wait_send()
+        for k in range(1, nz):
+            sum_copy(f, k).wait_send()
+
+
+def fused(tokens, out_grad, routes, gates, w_gate_up, w_down, plan, failed):
+    nz = lax.axis_size("grp")
+    ne = lax.axis_size("ep")
+    z = lax.axis_index("grp")
+    me = lax.axis_index("ep")
+    tok_count, model = tokens.shape
+    topk = routes.shape[1]
+    experts = ne // 2
+    capacity = tok_count * topk * 5 // (4 * ne)
+    block = -(-capacity // ROW_TILE) * ROW_TILE
+    count = ne * block
+    shard = w_gate_up.shape[1]
+    hidden_width = w_down.shape[2]
+    width = LANES
+    chunks = hidden_width // width
+    own_rows = model // (nz * ne)
+    in_service = 1 - lax.dynamic_index_in_dim(failed, z, 0, keepdims=False)
+    slot_index, slot_rank = assign(routes, plan, in_service, capacity, experts)
+    place = (lax.rem(slot_index - me + ne, ne) * block + slot_rank).reshape(tok_count, topk).T
+    spots = jnp.arange(count, dtype=jnp.int32)
+    pack = (spots[None, :, None] == place[:, None, :]).astype(jnp.bfloat16)
+    unpack = (spots[None, None, :] == place[:, :, None]).astype(jnp.bfloat16)
+    gate_wide = jnp.broadcast_to(gates.T[:, :, None], (topk, tok_count, LANES))
+    source = lax.rem(me - jnp.arange(ne, dtype=jnp.int32) + ne, ne)
+    hosted = (plan[None, :] == jnp.arange(experts, dtype=jnp.int32)[:, None]) & (
+        in_service[None, :] > 0
+    )
+    mask = hosted.astype(jnp.float32)[:, source]
+    bf16, f32 = jnp.bfloat16, jnp.float32
+    vmem = pl.BlockSpec(memory_space=pltpu.VMEM)
+    dma = pltpu.SemaphoreType.DMA
+    tgrad, ggrad, wgrad = pl.pallas_call(
+        functools.partial(fused_kernel, nz, ne, block),
+        out_shape=(
+            jax.ShapeDtypeStruct((tok_count, model), bf16),
+            jax.ShapeDtypeStruct((tok_count, LANES), bf16),
+            jax.ShapeDtypeStruct((experts, own_rows, 3 * hidden_width), f32),
+        ),
+        in_specs=[vmem] * 7 + [pl.BlockSpec(memory_space=pltpu.SMEM)],
+        out_specs=(vmem, vmem, vmem),
+        scratch_shapes=[
+            pltpu.VMEM((chunks, nz, shard, 3 * width), bf16),
+            pltpu.VMEM((count, 2 * model + LANES), bf16),
+            pltpu.VMEM((count, 2 * model + LANES), bf16),
+            pltpu.VMEM((model, count), bf16),
+            pltpu.VMEM((model, count), bf16),
+            pltpu.VMEM((count, model), f32),
+            pltpu.VMEM((count, width), f32),
+            pltpu.VMEM((chunks, ne, nz, own_rows, 3 * width), bf16),
+            pltpu.VMEM((chunks, ne, nz, own_rows, 3 * width), bf16),
+            pltpu.VMEM((chunks, nz, experts, own_rows, 3 * width), bf16),
+            pltpu.VMEM((chunks, nz, experts, own_rows, 3 * width), bf16),
+            pltpu.VMEM((count, model + LANES), bf16),
+            pltpu.VMEM((count, model + LANES), bf16),
+            dma((chunks, nz, 2)),
+            dma((chunks, nz)),
+            dma((ne,)),
+            dma((ne,)),
+            dma((chunks, ne)),
+            dma((chunks, ne)),
+            dma((chunks, nz)),
+            dma((chunks, nz)),
+            dma((ne,)),
+            dma((ne,)),
+        ],
+        compiler_params=pltpu.CompilerParams(
+            collective_id=0, has_side_effects=True, vmem_limit_bytes=60 * 1024 * 1024
+        ),
+        cost_estimate=pl.CostEstimate(
+            flops=18 * count * model * hidden_width,
+            bytes_accessed=16 * 1024 * 1024,
+            transcendentals=count * hidden_width,
+        ),
+    )(tokens, out_grad, pack, unpack, gate_wide, w_gate_up, w_down, mask)
+    return (tgrad, ggrad[:, :topk], wgrad)
+
+
 def local(tokens, out_grad, routes, gates, w_gate_up, w_down, plan, failed):
     groups = lax.axis_size("grp")
     slot_count = lax.axis_size("ep")
@@ -70,7 +483,8 @@
     route_count = tok_count * topk_count
     buffer_rows = slot_count * capacity
     in_service = 1 - lax.dynamic_index_in_dim(failed, my_group, 0, keepdims=False)
-    positions = assign(routes, plan, in_service, capacity, experts)
+    slot_index, slot_rank = assign(routes, plan, in_service, capacity, experts)
+    positions = slot_index * capacity + slot_rank
     source = (
         jnp.full((buffer_rows,), route_count, jnp.int32)
         .at[positions]
@@ -142,6 +556,12 @@
 
 
 def solution(mesh):
+    nz, ne = mesh.shape["grp"], mesh.shape["ep"]
+
+    def step(tokens, *others):
+        aligned = tokens.shape[1] % (nz * ne * ROW_TILE) == 0
+        return (fused if aligned else local)(tokens, *others)
+
     placed = (
         P(("grp", "ep"), None),
         P(("grp", "ep"), None),
@@ -153,7 +573,7 @@
         P(),
     )
     return jax.shard_map(
-        local,
+        step,
         mesh=mesh,
         in_specs=placed,
         out_specs=(P(("grp", "ep"), None), P(("grp", "ep"), None), P(None, ("grp", "ep"), None)),

time: 419 us -> 197 us (0.47)
  waiting for transfers between devices: 302 us -> 0 us
  Pallas kernels: 0 us -> 178 us
  starting transfers between devices: 30.2 us -> 0 us
  matrix products: 27 us -> 0 us
  local copies, waits for them, and re-layouts: 35.8 us -> 10.4 us
  between operations: 14.4 us -> 0.71 us
    all_to_all x7 -> x0, waiting for transfers between devices: 238 us -> none  [the longest x1 134 us: local(): lax.all_to_all(slot_grad, 'grp', split_axis=0, concat_axis=0, tiled=True)]
    pallas_call x0 -> x1, Pallas kernels: none -> 178 us  [fused(): pl.pallas_call(functools.partial(fused_kernel, nz, ne, block), out_shape=...]
    all_gather x2 -> x0, waiting for transfers between devices: 62.3 us -> none  [the longest x1 41.3 us: local(): lax.all_gather(w_down, 'grp', axis=1, tiled=True)]
    all_to_all x7 -> x0, starting transfers between devices: 30.1 us -> none  [the longest x1 5.37 us: local(): lax.all_to_all(slot_grad, 'grp', split_axis=0, concat_axis=0, tiled=True)]
    dot_general x7 -> x0, matrix products: 27 us -> none  [the longest x1 6.6 us: local(): jnp.einsum('ges,gsrc->gerc', hosted_all, mixed, preferred_element_type=jn...]
    all_to_all x2 -> x0, local copies, waits for them, and re-layouts: 11 us -> none  [the longest x1 10.3 us: local(): lax.all_to_all(slot_grad, 'grp', split_axis=0, concat_axis=0, tiled=True)]
    gather x5 -> x2, local copies, waits for them, and re-layouts: 11.8 us -> 1.22 us  [fused(): mask = hosted.astype(jnp.float32)[:, source]]
  transfers between devices with their start and end apart: 9 -> 0, of which waited for: 8 -> 0; matrix products, arithmetic and copies ran while one was open for 14% -> 0% of each run, Pallas kernels for 0% -> 0%
where the time goes in v1:
time: 197 us
  Pallas kernels  178 us (90%)
  local copies, waits for them, and re-layouts  10.4 us (5%)
  other arithmetic  7.62 us (4%)
    pallas_call x1, Pallas kernels, fused(): pl.pallas_call(functools.partial(fused_kernel, nz, ne, block), out_shape=...  178 us
    unnamed x4, local copies, waits for them, and re-layouts  6.67 us

profile of v1, /device:TPU:0, one launch (start us, length us, event | category | flops | bytes accessed | tf_op | source)
XLA Modules:
  0.0 196.9 jit_solution(2396109259230052539)
XLA Ops:
  0.6 0.7 compare_bitcast_fusion
  1.4 0.7 fusion.10
  2.1 0.6 gather_fusion
  2.6 0.7 copy.21
  3.3 0.8 select_reduce_fusion.2
  4.2 0.8 copy.15
  5.0 0.1 eq.136
  5.1 0.1 eq.126
  5.3 1.2 reduce-window.14
  7.0 0.1 and_select_fusion
  7.1 0.1 and_select_fusion.1
  7.2 0.7 and_convert_fusion
  8.0 0.6 reduce-window.16
  8.5 0.2 slice_reduce_fusion
  8.8 0.8 select_reduce_fusion
  9.5 0.1 add.56
  9.7 0.1 reduce_sum.68
  9.9 1.4 broadcast_in_dim.10.gate_ref
  11.3 0.8 fusion.1.unpack_ref
  12.1 0.7 fusion.pack_ref
  12.8 178.1 %shard_map.103 = (bf16[128,2048]{1,0:T(8,128)(2,1)}, bf16[128,128]{1,0:T(8,128)(2,1)}, f32[4,64,1536]{2,1,0:T(8,128)}) custom-call(bf16[128,2048]{1,0:T(8,128)(2,1)} %tok_ref.1, bf16[128,2048]{1,0:T(8,128)(2,1)} %dy_ref.1, bf16[2,384,128]{2,1,0:T(8,128)(2,1)} %fusion.pack_ref, bf16[2,128,384]{2,1,0:T(8,128)(2,1)} %fusion.1.unpack_ref, ...), custom_call_target="tpu_custom_call" | custom-call | flops 7247757312 | bytes 16777216 | tf_op jit(solution)/shard_map/pallas_call | solution.py:429
  191.0 1.4 copy.22
  192.3 1.9 copy.27
  194.2 2.7 %copy.28 = f32[4,64,1536]{2,1,0:T(8,128)} copy(f32[4,64,1536]{2,1,0:T(8,128)} %get-tuple-element.28) | data formatting | bytes 3145728
  (16 shorter events, 0.7 us)

commit v2 on v1

--- a/solution.py
+++ b/solution.py
@@ -70,10 +70,10 @@
 
 def fused_kernel(
     nz, ne, block,
-    tok_ref, dy_ref, pack_ref, unpack_ref, gate_ref, gu_ref, dn_ref, mask_ref,
+    tok_ref, dy_ref, route_ref, gate_ref, gu_ref, dn_ref, plan_ref, failed_ref,
     tgrad_ref, ggrad_ref, wgrad_ref,
     weights, send_rows, rows, x_t, dy_t, row_acc, gate_acc, slot_grads, peer_grads,
-    plane_sums, far_sums, ret, back,
+    plane_sums, from_below, from_above, ret, back, pack_ref, unpack_ref,
     ag_send, ag_recv, out_send, out_recv, grad_send, grad_recv, sum_send, sum_recv,
     ret_send, ret_recv,
 ):
@@ -98,13 +98,14 @@
             barrier, inc=1, device_id={"grp": lax.rem(z + k, nz)}, device_id_type=MESH
         )
 
-    for f in range(chunks):
+    def stage(f):
         cols = slice(f * width, (f + 1) * width)
+        up_cols = slice(hidden_width + f * width, hidden_width + (f + 1) * width)
         weights[f, z, :, 0:width] = gu_ref[0, :, cols]
-        weights[f, z, :, width : 2 * width] = gu_ref[
-            0, :, hidden_width + f * width : hidden_width + (f + 1) * width
-        ]
+        weights[f, z, :, width : 2 * width] = gu_ref[0, :, up_cols]
         weights[f, z, :, 2 * width : 3 * width] = dn_ref[0, :, cols]
+
+    stage(0)
     pl.semaphore_wait(barrier, ne - 1 + nz - 1)
 
     def shard_copy(f, owner, up):
@@ -179,8 +180,8 @@
             both, dy_ref[...], preferred_element_type=f32
         ).astype(bf16)
         target[here, 2 * model : 2 * model + LANES] = (
-            jnp.dot(first, gate_ref[0], preferred_element_type=f32)
-            + jnp.dot(second, gate_ref[1], preferred_element_type=f32)
+            jnp.dot(first, gate_wide[0], preferred_element_type=f32)
+            + jnp.dot(second, gate_wide[1], preferred_element_type=f32)
         ).astype(bf16)
 
     def grad_copy(f, k):
@@ -193,15 +194,36 @@
             device_id_type=MESH,
         )
 
-    def sum_copy(f, k):
+    def sum_copy(f, dest, up):
+        step = 1 if up else nz - 1
+        target = from_below if up else from_above
         return pltpu.make_async_remote_copy(
-            src_ref=plane_sums.at[f, lax.rem(z + k, nz)],
-            dst_ref=far_sums.at[f, k],
-            send_sem=sum_send.at[f, k],
-            recv_sem=sum_recv.at[f, k],
-            device_id={"grp": lax.rem(z + k, nz)},
+            src_ref=plane_sums.at[f, dest],
+            dst_ref=target.at[f, dest],
+            send_sem=sum_send.at[f, dest],
+            recv_sem=sum_recv.at[f, dest, 0 if up else 1],
+            device_id={"grp": lax.rem(z + step, nz)},
             device_id_type=MESH,
         )
+
+    def sum_hop(f, turn):
+        for up in (True, False):
+            dest = nz - 1 - turn if up else turn
+            incoming = from_below if up else from_above
+
+            @pl.when((z > 0) & (z < dest) if up else (z < nz - 1) & (z > dest))
+            def _():
+                sum_copy(f, dest, up).wait_recv()
+
+                @pl.loop(0, experts)
+                def _(e):
+                    plane_sums[f, dest, e] = (
+                        plane_sums[f, dest, e].astype(f32) + incoming[f, dest, e].astype(f32)
+                    ).astype(bf16)
+
+            @pl.when(z < dest if up else z > dest)
+            def _():
+                sum_copy(f, dest, up).start()
 
     def ret_copy(k):
         return pltpu.make_async_remote_copy(
@@ -279,33 +301,103 @@
                     else:
                         value = peer_grads[f, k, g, here, :].astype(f32)
                     for e in range(experts):
-                        term = value * mask_ref[e, k]
+                        term = value * mask[e][k]
                         total[e] = term if total[e] is None else total[e] + term
                 for e in range(experts):
                     plane_sums[f, g, e, here, :] = total[e].astype(bf16)
 
-        for k in range(1, nz):
-            sum_copy(f, k).start()
-
     def finish(f):
-        for k in range(1, nz):
-            sum_copy(f, k).wait_recv()
-
-        @pl.loop(0, experts)
-        def _(e):
-            total = plane_sums[f, z, e].astype(f32)
-            for k in range(1, nz):
-                total = total + far_sums[f, k, e].astype(f32)
-            total = total / nz
-            for part in range(3):
-                start = part * hidden_width + f * width
-                wgrad_ref[e, :, start : start + width] = total[
-                    :, part * width : (part + 1) * width
-                ]
+        def add(incoming, first):
+            @pl.loop(0, experts)
+            def _(e):
+                value = incoming[f, z, e].astype(f32)
+                if first:
+                    value = value + plane_sums[f, z, e].astype(f32)
+                for part in range(3):
+                    start = part * hidden_width + f * width
+                    here = value[:, part * width : (part + 1) * width] / nz
+                    if first:
+                        wgrad_ref[e, :, start : start + width] = here
+                    else:
+                        wgrad_ref[e, :, start : start + width] += here
+
+        @pl.when(z > 0)
+        def _():
+            sum_copy(f, z, True).wait_recv()
+            add(from_below, True)
+
+        @pl.when((z > 0) & (z < nz - 1))
+        def _():
+            sum_copy(f, z, False).wait_recv()
+            add(from_above, False)
+
+        @pl.when(z == 0)
+        def _():
+            sum_copy(f, z, False).wait_recv()
+            add(from_above, True)
 
     start_own(0)
+    for f in range(1, chunks):
+        stage(f)
     if chunks > 1:
         start_own(1)
+
+    live = [1 - failed_ref[z, s] for s in range(ne)]
+    tokens_here = tok_ref.shape[0]
+    square = (tokens_here, LANES)
+    lane = lax.broadcasted_iota(jnp.int32, square, 1)
+    hosts_row = lax.broadcasted_iota(jnp.int32, (LANES, LANES), 0)
+    hosts_lane = lax.broadcasted_iota(jnp.int32, (LANES, LANES), 1)
+    hosts = jnp.zeros((LANES, LANES), f32)
+    replicas = jnp.zeros(square, f32)
+    ordinal = jnp.zeros(square, f32)
+    for s in range(ne):
+        served = live[s].astype(f32)
+        hosts += jnp.where(
+            (hosts_row == plan_ref[s]) & (hosts_lane == s), served, 0.0
+        )
+        replicas += jnp.where(lane == plan_ref[s], served, 0.0)
+        before = jnp.int32(0)
+        for other in range(s):
+            before += (plan_ref[other] == plan_ref[s]).astype(jnp.int32) * live[other]
+        ordinal += jnp.where(lane == s, before.astype(f32), 0.0)
+    hosts = hosts.astype(bf16)
+    earlier = (
+        lax.broadcasted_iota(jnp.int32, (tokens_here, tokens_here), 1)
+        < lax.broadcasted_iota(jnp.int32, (tokens_here, tokens_here), 0)
+    ).astype(f32).astype(bf16)
+    wanted = [
+        (lane == route_ref[:, k : k + 1]).astype(f32) for k in range(2)
+    ]
+    ranks = jnp.dot(earlier, (wanted[0] + wanted[1]).astype(bf16), preferred_element_type=f32)
+    chosen = []
+    for k in range(2):
+        rank = jnp.sum(wanted[k] * ranks, axis=1, keepdims=True)
+        n = jnp.sum(wanted[k] * replicas, axis=1, keepdims=True)
+        pick = rank - n * jnp.floor((rank + 0.5) / n)
+        hosting = jnp.dot(wanted[k].astype(bf16), hosts, preferred_element_type=f32)
+        chosen.append(jnp.where(jnp.abs(ordinal - pick) < 0.5, hosting, 0.0))
+    places = jnp.dot(earlier, (chosen[0] + chosen[1]).astype(bf16), preferred_element_type=f32)
+    offset = (lax.rem(lane - me + ne, ne) * block).astype(f32)
+    spot = lax.broadcasted_iota(jnp.int32, (tokens_here, count), 1)
+    gate_wide = []
+    for k in range(2):
+        place = jnp.sum(
+            jnp.where(lane < ne, chosen[k] * (places + offset), 0.0), axis=1, keepdims=True
+        )
+        hot = (spot == place.astype(jnp.int32)).astype(f32)
+        unpack_ref[k] = hot.astype(bf16)
+        pack_ref[k] = hot.T.astype(bf16)
+        gate_wide.append(
+            jnp.broadcast_to(gate_ref[:, k : k + 1].astype(f32), square).astype(bf16)
+        )
+    mask = []
+    for e in range(experts):
+        mask.append([])
+        for k in range(ne):
+            slot = lax.rem(me - k + ne, ne)
+            hosted = (plan_ref[slot] == e).astype(jnp.int32) * (1 - failed_ref[z, slot])
+            mask[e].append(hosted.astype(f32))
 
     @pl.loop(1, ne)
     def _(k):
@@ -329,24 +421,33 @@
         for hop in range(low, min(high, nz)):
             arrive(f, hop)
 
-    late = chunks > 1 and nz > 2
+    turns = nz - 1
+    duties = []
+
+    def sums(f):
+        return [functools.partial(plane_sum, f)] + [
+            functools.partial(sum_hop, f, turn) for turn in range(turns)
+        ]
+
+    def work(most):
+        for _ in range(min(most, len(duties))):
+            duties.pop(0)()
+
     hop_range(0, 1, nz)
-    if not late:
-        rows_ready()
-        compute(0)
     for f in range(1, chunks):
         if f + 1 < chunks:
             start_own(f + 1)
-        if f == 1 and late:
-            hop_range(1, 1, nz - 1)
+        hop_range(f, 1, 2)
+        work(1)
+        hop_range(f, 2, nz - 1)
+        if f == 1:
             rows_ready()
             compute(0)
-            hop_range(1, nz - 1, nz)
         else:
-            hop_range(f, 1, nz - 1)
-            if f >= 2:
-                plane_sum(f - 2)
-            hop_range(f, nz - 1, nz)
+            duties += sums(f - 2)
+            work(2)
+        hop_range(f, max(2, nz - 1), nz)
+        work(1)
         compute(f)
 
     ret[:, model : model + LANES] = jnp.broadcast_to(
@@ -355,11 +456,14 @@
     for k in range(1, ne):
         ret_copy(k).start()
     back[0:block, :] = ret[0:block, :]
-    if chunks > 1:
-        plane_sum(chunks - 2)
-    for f in range(chunks - 2):
+    work(len(duties))
+    for f in range(max(chunks - 2, 0), chunks - 1):
+        for duty in sums(f):
+            duty()
+    for f in range(chunks - 1):
         finish(f)
-    plane_sum(chunks - 1)
+    for duty in sums(chunks - 1):
+        duty()
 
     for k in range(1, ne):
         ret_copy(k).wait_recv()
@@ -374,15 +478,13 @@
         ).astype(bf16)
 
     gates_back = back[:, model : model + LANES]
-    lane = lax.broadcasted_iota(jnp.int32, ggrad_ref.shape, 1)
     ggrad_ref[...] = jnp.where(
         lane == 0,
         jnp.dot(first, gates_back, preferred_element_type=f32),
         jnp.dot(second, gates_back, preferred_element_type=f32),
     ).astype(bf16)
 
-    for f in range(max(chunks - 2, 0), chunks):
-        finish(f)
+    finish(chunks - 1)
 
     shard_sends_done()
     for k in range(1, ne):
@@ -391,15 +493,16 @@
     for f in range(chunks):
         for k in range(1, ne):
             grad_copy(f, k).wait_send()
-        for k in range(1, nz):
-            sum_copy(f, k).wait_send()
+        for dest in range(nz):
+            for up in (True, False):
+                @pl.when(z < dest if up else z > dest)
+                def _():
+                    sum_copy(f, dest, up).wait_send()
 
 
 def fused(tokens, out_grad, routes, gates, w_gate_up, w_down, plan, failed):
     nz = lax.axis_size("grp")
     ne = lax.axis_size("ep")
-    z = lax.axis_index("grp")
-    me = lax.axis_index("ep")
     tok_count, model = tokens.shape
     topk = routes.shape[1]
     experts = ne // 2
@@ -411,18 +514,6 @@
     width = LANES
     chunks = hidden_width // width
     own_rows = model // (nz * ne)
-    in_service = 1 - lax.dynamic_index_in_dim(failed, z, 0, keepdims=False)
-    slot_index, slot_rank = assign(routes, plan, in_service, capacity, experts)
-    place = (lax.rem(slot_index - me + ne, ne) * block + slot_rank).reshape(tok_count, topk).T
-    spots = jnp.arange(count, dtype=jnp.int32)
-    pack = (spots[None, :, None] == place[:, None, :]).astype(jnp.bfloat16)
-    unpack = (spots[None, None, :] == place[:, :, None]).astype(jnp.bfloat16)
-    gate_wide = jnp.broadcast_to(gates.T[:, :, None], (topk, tok_count, LANES))
-    source = lax.rem(me - jnp.arange(ne, dtype=jnp.int32) + ne, ne)
-    hosted = (plan[None, :] == jnp.arange(experts, dtype=jnp.int32)[:, None]) & (
-        in_service[None, :] > 0
-    )
-    mask = hosted.astype(jnp.float32)[:, source]
     bf16, f32 = jnp.bfloat16, jnp.float32
     vmem = pl.BlockSpec(memory_space=pltpu.VMEM)
     dma = pltpu.SemaphoreType.DMA
@@ -433,7 +524,7 @@
             jax.ShapeDtypeStruct((tok_count, LANES), bf16),
             jax.ShapeDtypeStruct((experts, own_rows, 3 * hidden_width), f32),
         ),
-        in_specs=[vmem] * 7 + [pl.BlockSpec(memory_space=pltpu.SMEM)],
+        in_specs=[vmem] * 6 + [pl.BlockSpec(memory_space=pltpu.SMEM)] * 2,
         out_specs=(vmem, vmem, vmem),
         scratch_shapes=[
             pltpu.VMEM((chunks, nz, shard, 3 * width), bf16),
@@ -447,8 +538,11 @@
             pltpu.VMEM((chunks, ne, nz, own_rows, 3 * width), bf16),
             pltpu.VMEM((chunks, nz, experts, own_rows, 3 * width), bf16),
             pltpu.VMEM((chunks, nz, experts, own_rows, 3 * width), bf16),
+            pltpu.VMEM((chunks, nz, experts, own_rows, 3 * width), bf16),
             pltpu.VMEM((count, model + LANES), bf16),
             pltpu.VMEM((count, model + LANES), bf16),
+            pltpu.VMEM((topk, count, tok_count), bf16),
+            pltpu.VMEM((topk, tok_count, count), bf16),
             dma((chunks, nz, 2)),
             dma((chunks, nz)),
             dma((ne,)),
@@ -456,7 +550,7 @@
             dma((chunks, ne)),
             dma((chunks, ne)),
             dma((chunks, nz)),
-            dma((chunks, nz)),
+            dma((chunks, nz, 2)),
             dma((ne,)),
             dma((ne,)),
         ],
@@ -468,7 +562,7 @@
             bytes_accessed=16 * 1024 * 1024,
             transcendentals=count * hidden_width,
         ),
-    )(tokens, out_grad, pack, unpack, gate_wide, w_gate_up, w_down, mask)
+    )(tokens, out_grad, routes, gates, w_gate_up, w_down, plan, failed)
     return (tgrad, ggrad[:, :topk], wgrad)
 
 

time: 197 us -> 192 us (0.975); the launches traced: 197 us -> 189 us
  other arithmetic: 7.62 us -> 0 us
    convert_element_type x5 -> x0, other arithmetic: 2.97 us -> none  [the longest x1 0.78 us: fused(): unpack = (spots[None, None, :] == place[:, :, None]).astype(jnp.bfloat16)]
    unnamed x4 -> x5, local copies, waits for them, and re-layouts: 6.67 us -> 8.68 us
where the time goes in v2:
time: 192 us; the launch traced here: 189 us
  Pallas kernels  179 us (93%)
  local copies, waits for them, and re-layouts  8.68 us (5%)
    pallas_call x1, Pallas kernels, fused(): pl.pallas_call(functools.partial(fused_kernel, nz, ne, block), out_shape=...  179 us
    unnamed x5, local copies, waits for them, and re-layouts  8.68 us

profile of v2, /device:TPU:0, one launch (start us, length us, event | category | flops | bytes accessed | tf_op | source)
XLA Modules:
  0.0 188.7 jit_solution(251458157343577032)
XLA Ops:
  0.6 1.4 copy.12.gate_ref
  2.0 1.4 copy.11.route_ref
  3.4 179.4 %shard_map.103 = (bf16[128,2048]{1,0:T(8,128)(2,1)}, bf16[128,128]{1,0:T(8,128)(2,1)}, f32[4,64,1536]{2,1,0:T(8,128)}) custom-call(bf16[128,2048]{1,0:T(8,128)(2,1)} %tok_ref.1, bf16[128,2048]{1,0:T(8,128)(2,1)} %dy_ref.1, s32[128,2]{1,0:T(8,128)} %copy.11.route_ref, bf16[128,2]{1,0:T(8,128)(2,1)} %copy.12.gate_ref, bf16[1,512,1024]{2,1,0:T(8,128)(2,1)} %gu_ref.1, ...), custom_call_target="tpu_custom_call" | custom-call | flops 7247757312 | bytes 16777216 | tf_op jit(solution)/shard_map/pallas_call | solution.py:520
  182.8 1.4 copy.13
  184.2 1.9 copy.16
  186.0 2.7 %copy.17 = f32[4,64,1536]{2,1,0:T(8,128)} copy(f32[4,64,1536]{2,1,0:T(8,128)} %get-tuple-element.17) | data formatting | bytes 3145728

commit v3 on v2

--- a/solution.py
+++ b/solution.py
@@ -87,6 +87,12 @@
     own_rows = wgrad_ref.shape[1]
     count = ne * block
     f32, bf16 = jnp.float32, jnp.bfloat16
+    last = chunks - 1
+    both_parts, gu_part, dn_part = (0, width3), (0, 2 * width), (2 * width, width3)
+    weight_pieces = [(f,) + both_parts for f in range(last)]
+    weight_pieces += [(last,) + gu_part, (last,) + dn_part]
+    grad_pieces = [(f,) + both_parts for f in range(last)]
+    grad_pieces += [(last,) + dn_part, (last,) + gu_part]
 
     barrier = pltpu.get_barrier_semaphore()
     for k in range(1, ne):
@@ -108,53 +114,54 @@
     stage(0)
     pl.semaphore_wait(barrier, ne - 1 + nz - 1)
 
-    def shard_copy(f, owner, up):
+    def shard_copy(p, owner, up):
         step = 1 if up else nz - 1
+        f, low, high = weight_pieces[p]
         return pltpu.make_async_remote_copy(
-            src_ref=weights.at[f, owner],
-            dst_ref=weights.at[f, owner],
-            send_sem=ag_send.at[f, owner, 0 if up else 1],
-            recv_sem=ag_recv.at[f, owner],
+            src_ref=weights.at[f, owner, :, low:high],
+            dst_ref=weights.at[f, owner, :, low:high],
+            send_sem=ag_send.at[p, owner, 0 if up else 1],
+            recv_sem=ag_recv.at[p, owner],
             device_id={"grp": lax.rem(z + step, nz)},
             device_id_type=MESH,
         )
 
-    def start_own(f):
+    def start_own(p):
         @pl.when(z < nz - 1)
         def _():
-            shard_copy(f, z, True).start()
+            shard_copy(p, z, True).start()
 
         @pl.when(z > 0)
         def _():
-            shard_copy(f, z, False).start()
-
-    def arrive(f, hop):
+            shard_copy(p, z, False).start()
+
+    def arrive(p, hop):
         @pl.when(z >= hop)
         def _():
-            shard_copy(f, z - hop, True).wait_recv()
+            shard_copy(p, z - hop, True).wait_recv()
 
             @pl.when(z < nz - 1)
             def _():
-                shard_copy(f, z - hop, True).start()
+                shard_copy(p, z - hop, True).start()
 
         @pl.when(z + hop < nz)
         def _():
-            shard_copy(f, z + hop, False).wait_recv()
+            shard_copy(p, z + hop, False).wait_recv()
 
             @pl.when(z > 0)
             def _():
-                shard_copy(f, z + hop, False).start()
+                shard_copy(p, z + hop, False).start()
 
     def shard_sends_done():
-        for f in range(chunks):
+        for p in range(len(weight_pieces)):
             for hop in range(nz):
                 @pl.when((z >= hop) & (z < nz - 1))
                 def _():
-                    shard_copy(f, z - hop, True).wait_send()
+                    shard_copy(p, z - hop, True).wait_send()
 
                 @pl.when((z + hop < nz) & (z > 0))
                 def _():
-                    shard_copy(f, z + hop, False).wait_send()
+                    shard_copy(p, z + hop, False).wait_send()
 
     def block_rows(k):
         return pl.ds(pl.multiple_of(k * block, ROW_TILE), block)
@@ -184,46 +191,69 @@
             + jnp.dot(second, gate_wide[1], preferred_element_type=f32)
         ).astype(bf16)
 
-    def grad_copy(f, k):
+    def grad_copy(q, k):
+        f, low, high = grad_pieces[q]
         return pltpu.make_async_remote_copy(
-            src_ref=slot_grads.at[f, lax.rem(me + k, ne)],
-            dst_ref=peer_grads.at[f, k],
-            send_sem=grad_send.at[f, k],
-            recv_sem=grad_recv.at[f, k],
+            src_ref=slot_grads.at[f, lax.rem(me + k, ne), :, :, low:high],
+            dst_ref=peer_grads.at[f, k, :, :, low:high],
+            send_sem=grad_send.at[q, k],
+            recv_sem=grad_recv.at[q, k],
             device_id={"ep": lax.rem(me + k, ne)},
             device_id_type=MESH,
         )
 
-    def sum_copy(f, dest, up):
+    def sum_copy(q, dest, up):
         step = 1 if up else nz - 1
         target = from_below if up else from_above
+        f, low, high = grad_pieces[q]
         return pltpu.make_async_remote_copy(
-            src_ref=plane_sums.at[f, dest],
-            dst_ref=target.at[f, dest],
-            send_sem=sum_send.at[f, dest],
-            recv_sem=sum_recv.at[f, dest, 0 if up else 1],
+            src_ref=plane_sums.at[f, dest, :, :, low:high],
+            dst_ref=target.at[f, dest, :, :, low:high],
+            send_sem=sum_send.at[q, dest],
+            recv_sem=sum_recv.at[q, dest, 0 if up else 1],
             device_id={"grp": lax.rem(z + step, nz)},
             device_id_type=MESH,
         )
 
-    def sum_hop(f, turn):
+    def pass_on(q, dest, up, first):
+        f, low, high = grad_pieces[q]
+        incoming = from_below if up else from_above
+        if not first:
+            sum_copy(q, dest, up).wait_recv()
+
+            @pl.loop(0, experts)
+            def _(e):
+                plane_sums[f, dest, e, :, low:high] = (
+                    plane_sums[f, dest, e, :, low:high].astype(f32)
+                    + incoming[f, dest, e, :, low:high].astype(f32)
+                ).astype(bf16)
+
+        sum_copy(q, dest, up).start()
+
+    def sum_turn(q, turn):
         for up in (True, False):
             dest = nz - 1 - turn if up else turn
-            incoming = from_below if up else from_above
-
-            @pl.when((z > 0) & (z < dest) if up else (z < nz - 1) & (z > dest))
+            edge = z == 0 if up else z == nz - 1
+            short = z < dest if up else z > dest
+
+            @pl.when(short & edge)
             def _():
-                sum_copy(f, dest, up).wait_recv()
-
-                @pl.loop(0, experts)
-                def _(e):
-                    plane_sums[f, dest, e] = (
-                        plane_sums[f, dest, e].astype(f32) + incoming[f, dest, e].astype(f32)
-                    ).astype(bf16)
-
-            @pl.when(z < dest if up else z > dest)
+                pass_on(q, dest, up, True)
+
+            @pl.when(short & jnp.logical_not(edge))
             def _():
-                sum_copy(f, dest, up).start()
+                pass_on(q, dest, up, False)
+
+    def sum_level(q, level):
+        @pl.when(z == level)
+        def _():
+            for dest in range(nz - 1, level, -1):
+                pass_on(q, dest, True, level == 0)
+
+        @pl.when(z == nz - 1 - level)
+        def _():
+            for dest in range(nz - 1 - level):
+                pass_on(q, dest, False, level == 0)
 
     def ret_copy(k):
         return pltpu.make_async_remote_copy(
@@ -235,18 +265,32 @@
             device_id_type=MESH,
         )
 
-    def compute(f):
+    def first_half(f):
         x = rows[:, 0:model]
+        gate = rows[:, 2 * model : 2 * model + LANES].astype(f32)
+        full = weights[f, :, :, 0 : 2 * width].reshape(model, 2 * width)
+        pre = jnp.dot(x, full, preferred_element_type=f32)
+        a, b = pre[:, :width], pre[:, width:]
+        sig = jax.nn.sigmoid(a)
+        hidden_f = (a * sig * b).astype(bf16).astype(f32)
+        gated = (gate * hidden_f).astype(bf16)
+
+        @pl.loop(0, nz)
+        def _(g):
+            here = pl.ds(pl.multiple_of(g * shard, shard), shard)
+            dn = jnp.dot(dy_t[here, :], gated, preferred_element_type=f32).astype(bf16)
+            slot_grads[f, :, g, :, 2 * width :] = dn.reshape(ne, own_rows, width)
+
+        if f == last:
+            for k in range(1, ne):
+                grad_copy(last, k).start()
+        return a, b, sig, hidden_f
+
+    def second_half(f, a, b, sig, hidden_f):
         dy = rows[:, model : 2 * model]
         gate = rows[:, 2 * model : 2 * model + LANES].astype(f32)
-        full = weights[f].reshape(model, width3)
-        pre = jnp.dot(x, full[:, 0 : 2 * width], preferred_element_type=f32)
-        upstream = jnp.dot(dy, full[:, 2 * width :], preferred_element_type=f32)
-        a, b = pre[:, :width], pre[:, width:]
-        sig = jax.nn.sigmoid(a)
-        silu = a * sig
-        hidden = (silu * b).astype(bf16)
-        hidden_f = hidden.astype(f32)
+        full = weights[f, :, :, 2 * width :].reshape(model, width)
+        upstream = jnp.dot(dy, full, preferred_element_type=f32)
         gate_part = upstream * hidden_f
         if f == 0:
             gate_acc[...] = gate_part
@@ -254,20 +298,17 @@
             gate_acc[...] += gate_part
         hidden_grad = gate * upstream
         da = hidden_grad * b * sig * (1.0 + a * (1.0 - sig))
-        db = hidden_grad * silu
+        db = hidden_grad * (a * sig)
         pre_grad = jnp.concatenate([da, db], axis=1).astype(bf16)
-        gated = (gate * hidden_f).astype(bf16)
 
         @pl.loop(0, nz)
         def _(g):
             here = pl.ds(pl.multiple_of(g * shard, shard), shard)
             gu = jnp.dot(x_t[here, :], pre_grad, preferred_element_type=f32).astype(bf16)
-            dn = jnp.dot(dy_t[here, :], gated, preferred_element_type=f32).astype(bf16)
             slot_grads[f, :, g, :, 0 : 2 * width] = gu.reshape(ne, own_rows, 2 * width)
-            slot_grads[f, :, g, :, 2 * width :] = dn.reshape(ne, own_rows, width)
 
         for k in range(1, ne):
-            grad_copy(f, k).start()
+            grad_copy(f + 1 if f == last else f, k).start()
 
         @pl.loop(0, nz)
         def _(g):
@@ -280,14 +321,20 @@
             )
             if f == 0:
                 row_acc[:, here] = part
-            elif f < chunks - 1:
+            elif f < last:
                 row_acc[:, here] += part
             else:
                 ret[:, here] = (row_acc[:, here] + part).astype(bf16)
 
-    def plane_sum(f):
+    def compute(f):
+        second_half(f, *first_half(f))
+
+    def grads_in(q):
         for k in range(1, ne):
-            grad_copy(f, k).wait_recv()
+            grad_copy(q, k).wait_recv()
+
+    def plane_sum(q):
+        f, low, high = grad_pieces[q]
 
         @pl.loop(0, nz)
         def _(g):
@@ -297,25 +344,27 @@
                 total = [None] * experts
                 for k in range(ne):
                     if k == 0:
-                        value = slot_grads[f, me, g, here, :].astype(f32)
+                        value = slot_grads[f, me, g, here, low:high].astype(f32)
                     else:
-                        value = peer_grads[f, k, g, here, :].astype(f32)
+                        value = peer_grads[f, k, g, here, low:high].astype(f32)
                     for e in range(experts):
                         term = value * mask[e][k]
                         total[e] = term if total[e] is None else total[e] + term
                 for e in range(experts):
-                    plane_sums[f, g, e, here, :] = total[e].astype(bf16)
-
-    def finish(f):
+                    plane_sums[f, g, e, here, low:high] = total[e].astype(bf16)
+
+    def finish(q):
+        f, low, high = grad_pieces[q]
+
         def add(incoming, first):
             @pl.loop(0, experts)
             def _(e):
-                value = incoming[f, z, e].astype(f32)
+                value = incoming[f, z, e, :, low:high].astype(f32)
                 if first:
-                    value = value + plane_sums[f, z, e].astype(f32)
-                for part in range(3):
+                    value = value + plane_sums[f, z, e, :, low:high].astype(f32)
+                for part in range(low // width, high // width):
                     start = part * hidden_width + f * width
-                    here = value[:, part * width : (part + 1) * width] / nz
+                    here = value[:, part * width - low : (part + 1) * width - low] / nz
                     if first:
                         wgrad_ref[e, :, start : start + width] = here
                     else:
@@ -323,17 +372,17 @@
 
         @pl.when(z > 0)
         def _():
-            sum_copy(f, z, True).wait_recv()
+            sum_copy(q, z, True).wait_recv()
             add(from_below, True)
 
         @pl.when((z > 0) & (z < nz - 1))
         def _():
-            sum_copy(f, z, False).wait_recv()
+            sum_copy(q, z, False).wait_recv()
             add(from_above, False)
 
         @pl.when(z == 0)
         def _():
-            sum_copy(f, z, False).wait_recv()
+            sum_copy(q, z, False).wait_recv()
             add(from_above, True)
 
     start_own(0)
@@ -366,8 +415,12 @@
         lax.broadcasted_iota(jnp.int32, (tokens_here, tokens_here), 1)
         < lax.broadcasted_iota(jnp.int32, (tokens_here, tokens_here), 0)
     ).astype(f32).astype(bf16)
+
+    def column(ref, k):
+        return jnp.broadcast_to(ref[k : k + 1, :], (LANES, tokens_here)).T
+
     wanted = [
-        (lane == route_ref[:, k : k + 1]).astype(f32) for k in range(2)
+        (lane == column(route_ref, k)).astype(f32) for k in range(2)
     ]
     ranks = jnp.dot(earlier, (wanted[0] + wanted[1]).astype(bf16), preferred_element_type=f32)
     chosen = []
@@ -388,9 +441,8 @@
         hot = (spot == place.astype(jnp.int32)).astype(f32)
         unpack_ref[k] = hot.astype(bf16)
         pack_ref[k] = hot.T.astype(bf16)
-        gate_wide.append(
-            jnp.broadcast_to(gate_ref[:, k : k + 1].astype(f32), square).astype(bf16)
-        )
+        gate_row = jnp.broadcast_to(gate_ref[k : k + 1, :].astype(f32), (LANES, tokens_here))
+        gate_wide.append(gate_row.T.astype(bf16))
     mask = []
     for e in range(experts):
         mask.append([])
@@ -421,49 +473,64 @@
         for hop in range(low, min(high, nz)):
             arrive(f, hop)
 
-    turns = nz - 1
     duties = []
 
-    def sums(f):
-        return [functools.partial(plane_sum, f)] + [
-            functools.partial(sum_hop, f, turn) for turn in range(turns)
-        ]
-
-    def work(most):
-        for _ in range(min(most, len(duties))):
+    def work():
+        if duties:
             duties.pop(0)()
 
+    def first_level(q):
+        grads_in(q)
+        plane_sum(q)
+        sum_level(q, 0)
+
+    def levels(q):
+        duties.append(functools.partial(first_level, q))
+        for level in range(1, nz - 1):
+            duties.append(functools.partial(sum_level, q, level))
+
+    def hops_between(p):
+        for hop in range(1, nz):
+            arrive(p, hop)
+            work()
+
     hop_range(0, 1, nz)
-    for f in range(1, chunks):
-        if f + 1 < chunks:
-            start_own(f + 1)
-        hop_range(f, 1, 2)
-        work(1)
-        hop_range(f, 2, nz - 1)
+    for f in range(1, last):
+        start_own(f + 1)
         if f == 1:
+            hop_range(1, 1, nz - 1)
             rows_ready()
             compute(0)
+            hop_range(1, nz - 1, nz)
         else:
-            duties += sums(f - 2)
-            work(2)
-        hop_range(f, max(2, nz - 1), nz)
-        work(1)
+            levels(f - 2)
+            hops_between(f)
         compute(f)
-
+    start_own(last + 1)
+    levels(last - 2)
+    hops_between(last)
+    kept = first_half(last)
+    hops_between(last + 1)
+    second_half(last, *kept)
     ret[:, model : model + LANES] = jnp.broadcast_to(
         jnp.sum(gate_acc[...], axis=1, keepdims=True), (count, LANES)
     ).astype(bf16)
+    while duties:
+        work()
+    for q in (last - 1, last):
+        grads_in(q)
+        plane_sum(q)
+        for turn in range(nz - 1):
+            sum_turn(q, turn)
+    grads_in(last + 1)
     for k in range(1, ne):
         ret_copy(k).start()
+    plane_sum(last + 1)
+    for turn in range(nz - 1):
+        sum_turn(last + 1, turn)
+    for q in range(last + 1):
+        finish(q)
     back[0:block, :] = ret[0:block, :]
-    work(len(duties))
-    for f in range(max(chunks - 2, 0), chunks - 1):
-        for duty in sums(f):
-            duty()
-    for f in range(chunks - 1):
-        finish(f)
-    for duty in sums(chunks - 1):
-        duty()
 
     for k in range(1, ne):
         ret_copy(k).wait_recv()
@@ -484,20 +551,20 @@
         jnp.dot(second, gates_back, preferred_element_type=f32),
     ).astype(bf16)
 
-    finish(chunks - 1)
+    finish(last + 1)
 
     shard_sends_done()
     for k in range(1, ne):
         out_copy(k).wait_send()
         ret_copy(k).wait_send()
-    for f in range(chunks):
+    for q in range(len(grad_pieces)):
         for k in range(1, ne):
-            grad_copy(f, k).wait_send()
+            grad_copy(q, k).wait_send()
         for dest in range(nz):
             for up in (True, False):
                 @pl.when(z < dest if up else z > dest)
                 def _():
-                    sum_copy(f, dest, up).wait_send()
+                    sum_copy(q, dest, up).wait_send()
 
 
 def fused(tokens, out_grad, routes, gates, w_gate_up, w_down, plan, failed):
@@ -543,14 +610,14 @@
             pltpu.VMEM((count, model + LANES), bf16),
             pltpu.VMEM((topk, count, tok_count), bf16),
             pltpu.VMEM((topk, tok_count, count), bf16),
-            dma((chunks, nz, 2)),
-            dma((chunks, nz)),
+            dma((chunks + 1, nz, 2)),
+            dma((chunks + 1, nz)),
             dma((ne,)),
             dma((ne,)),
-            dma((chunks, ne)),
-            dma((chunks, ne)),
-            dma((chunks, nz)),
-            dma((chunks, nz, 2)),
+            dma((chunks + 1, ne)),
+            dma((chunks + 1, ne)),
+            dma((chunks + 1, nz)),
+            dma((chunks + 1, nz, 2)),
             dma((ne,)),
             dma((ne,)),
         ],
@@ -562,7 +629,7 @@
             bytes_accessed=16 * 1024 * 1024,
             transcendentals=count * hidden_width,
         ),
-    )(tokens, out_grad, routes, gates, w_gate_up, w_down, plan, failed)
+    )(tokens, out_grad, routes.T, gates.T, w_gate_up, w_down, plan, failed)
     return (tgrad, ggrad[:, :topk], wgrad)
 
 

time: 192 us -> 187 us (0.974)
  the two profiles are of different devices: /device:TPU:0 before, /device:TPU:8 now
where the time goes in v3:
time: 187 us
  Pallas kernels  180 us (96%)
  local copies, waits for them, and re-layouts  5.89 us (3%)
    pallas_call x1, Pallas kernels, fused(): pl.pallas_call(functools.partial(fused_kernel, nz, ne, block), out_shape=...  180 us
    unnamed x3, local copies, waits for them, and re-layouts  5.89 us

profile of v3, /device:TPU:8, one launch (start us, length us, event | category | flops | bytes accessed | tf_op | source)
XLA Modules:
  0.0 186.8 jit_solution(4837594924100582245)
XLA Ops:
  0.6 180.3 %shard_map.103 = (bf16[128,2048]{1,0:T(8,128)(2,1)}, bf16[128,128]{1,0:T(8,128)(2,1)}, f32[4,64,1536]{2,1,0:T(8,128)}) custom-call(bf16[128,2048]{1,0:T(8,128)(2,1)} %tok_ref.1, bf16[128,2048]{1,0:T(8,128)(2,1)} %dy_ref.1, s32[2,128]{1,0:T(2,128)} %bitcast.4, bf16[2,128]{1,0:T(2,128)(2,1)} %bitcast.5, bf16[1,512,1024]{2,1,0:T(8,128)(2,1)} %gu_ref.1, ...), custom_call_target="tpu_custom_call" | custom-call | flops 7247757312 | bytes 16777216 | tf_op jit(solution)/shard_map/pallas_call | solution.py:587
  180.9 1.4 copy.11
  182.3 1.9 %copy.14 = bf16[128,2048]{1,0:T(8,128)(2,1)} copy(bf16[128,2048]{1,0:T(8,128)(2,1)} %get-tuple-element.15) | data formatting | bytes 1048576
  184.1 2.7 %copy.15 = f32[4,64,1536]{2,1,0:T(8,128)} copy(f32[4,64,1536]{2,1,0:T(8,128)} %get-tuple-element.17) | data formatting | bytes 3145728

commit v4 on v3

--- a/solution.py
+++ b/solution.py
@@ -231,10 +231,12 @@
         sum_copy(q, dest, up).start()
 
     def sum_turn(q, turn):
-        for up in (True, False):
+        lower = 2 * z < nz
+
+        def serve(up, allowed):
             dest = nz - 1 - turn if up else turn
             edge = z == 0 if up else z == nz - 1
-            short = z < dest if up else z > dest
+            short = (z < dest if up else z > dest) & allowed
 
             @pl.when(short & edge)
             def _():
@@ -243,6 +245,10 @@
             @pl.when(short & jnp.logical_not(edge))
             def _():
                 pass_on(q, dest, up, False)
+
+        serve(False, jnp.logical_not(lower))
+        serve(True, z >= 0)
+        serve(False, lower)
 
     def sum_level(q, level):
         @pl.when(z == level)
@@ -309,7 +315,9 @@
 
         for k in range(1, ne):
             grad_copy(f + 1 if f == last else f, k).start()
-
+        return pre_grad
+
+    def row_part(f, pre_grad):
         @pl.loop(0, nz)
         def _(g):
             here = pl.ds(pl.multiple_of(g * shard, shard), shard)
@@ -327,7 +335,7 @@
                 ret[:, here] = (row_acc[:, here] + part).astype(bf16)
 
     def compute(f):
-        second_half(f, *first_half(f))
+        row_part(f, second_half(f, *first_half(f)))
 
     def grads_in(q):
         for k in range(1, ne):
@@ -509,26 +517,29 @@
     start_own(last + 1)
     levels(last - 2)
     hops_between(last)
+    first_level(last - 1)
     kept = first_half(last)
-    hops_between(last + 1)
-    second_half(last, *kept)
+    hop_range(last + 1, 1, nz)
+    pre_grad = second_half(last, *kept)
+    for level in range(1, nz - 2):
+        sum_level(last - 1, level)
+    row_part(last, pre_grad)
     ret[:, model : model + LANES] = jnp.broadcast_to(
         jnp.sum(gate_acc[...], axis=1, keepdims=True), (count, LANES)
     ).astype(bf16)
-    while duties:
-        work()
-    for q in (last - 1, last):
-        grads_in(q)
-        plane_sum(q)
-        for turn in range(nz - 1):
-            sum_turn(q, turn)
+    first_level(last)
+    sum_level(last - 1, nz - 2)
+    for level in range(1, nz - 1):
+        sum_level(last, level)
+    for q in range(last - 1):
+        finish(q)
     grads_in(last + 1)
     for k in range(1, ne):
         ret_copy(k).start()
     plane_sum(last + 1)
     for turn in range(nz - 1):
         sum_turn(last + 1, turn)
-    for q in range(last + 1):
+    for q in range(last - 1, last + 1):
         finish(q)
     back[0:block, :] = ret[0:block, :]
 
@@ -545,11 +556,12 @@
         ).astype(bf16)
 
     gates_back = back[:, model : model + LANES]
-    ggrad_ref[...] = jnp.where(
+    gate_grads = jnp.where(
         lane == 0,
         jnp.dot(first, gates_back, preferred_element_type=f32),
         jnp.dot(second, gates_back, preferred_element_type=f32),
-    ).astype(bf16)
+    )
+    ggrad_ref[...] = gate_grads.T[0:2, :].astype(bf16)
 
     finish(last + 1)
 
@@ -588,7 +600,7 @@
         functools.partial(fused_kernel, nz, ne, block),
         out_shape=(
             jax.ShapeDtypeStruct((tok_count, model), bf16),
-            jax.ShapeDtypeStruct((tok_count, LANES), bf16),
+            jax.ShapeDtypeStruct((topk, tok_count), bf16),
             jax.ShapeDtypeStruct((experts, own_rows, 3 * hidden_width), f32),
         ),
         in_specs=[vmem] * 6 + [pl.BlockSpec(memory_space=pltpu.SMEM)] * 2,
@@ -630,7 +642,7 @@
             transcendentals=count * hidden_width,
         ),
     )(tokens, out_grad, routes.T, gates.T, w_gate_up, w_down, plan, failed)
-    return (tgrad, ggrad[:, :topk], wgrad)
+    return (tgrad, ggrad.T, wgrad)
 
 
 def local(tokens, out_grad, routes, gates, w_gate_up, w_down, plan, failed):

time: 187 us -> 171 us (0.914)
  the two profiles are of different devices: /device:TPU:8 before, /device:TPU:0 now
where the time goes in v4:
time: 171 us
  Pallas kernels  164 us (96%)
  local copies, waits for them, and re-layouts  5.68 us (3%)
    pallas_call x1, Pallas kernels, fused(): pl.pallas_call(functools.partial(fused_kernel, nz, ne, block), out_shape=...  164 us
    unnamed x3, local copies, waits for them, and re-layouts  5.68 us

profile of v4, /device:TPU:0, one launch (start us, length us, event | category | flops | bytes accessed | tf_op | source)
XLA Modules:
  0.0 170.5 jit_solution(16665275633060376913)
XLA Ops:
  0.6 164.2 %shard_map.103 = (bf16[128,2048]{1,0:T(8,128)(2,1)}, bf16[2,128]{1,0:T(2,128)(2,1)}, f32[4,64,1536]{2,1,0:T(8,128)}) custom-call(bf16[128,2048]{1,0:T(8,128)(2,1)} %tok_ref.1, bf16[128,2048]{1,0:T(8,128)(2,1)} %dy_ref.1, s32[2,128]{1,0:T(2,128)} %bitcast.3, bf16[2,128]{1,0:T(2,128)(2,1)} %bitcast.4, bf16[1,512,1024]{2,1,0:T(8,128)(2,1)} %gu_ref.1, ...), custom_call_target="tpu_custom_call" | custom-call | flops 7247757312 | bytes 16777216 | tf_op jit(solution)/shard_map/pallas_call | solution.py:599
  164.8 1.9 %copy.14 = bf16[128,2048]{1,0:T(8,128)(2,1)} copy(bf16[128,2048]{1,0:T(8,128)(2,1)} %get-tuple-element.12) | data formatting | bytes 1048576
  166.7 1.1 copy.15
  167.8 2.7 %copy.16 = f32[4,64,1536]{2,1,0:T(8,128)} copy(f32[4,64,1536]{2,1,0:T(8,128)} %get-tuple-element.14) | data formatting | bytes 3145728

commit v5 on v4

--- a/solution.py
+++ b/solution.py
@@ -337,8 +337,8 @@
     def compute(f):
         row_part(f, second_half(f, *first_half(f)))
 
-    def grads_in(q):
-        for k in range(1, ne):
+    def grads_in(q, low=1, high=ne):
+        for k in range(low, high):
             grad_copy(q, k).wait_recv()
 
     def plane_sum(q):
@@ -494,7 +494,7 @@
 
     def levels(q):
         duties.append(functools.partial(first_level, q))
-        for level in range(1, nz - 1):
+        for level in range(1, nz - 2):
             duties.append(functools.partial(sum_level, q, level))
 
     def hops_between(p):
@@ -521,6 +521,8 @@
     kept = first_half(last)
     hop_range(last + 1, 1, nz)
     pre_grad = second_half(last, *kept)
+    for q in range(last - 1):
+        sum_level(q, nz - 2)
     for level in range(1, nz - 2):
         sum_level(last - 1, level)
     row_part(last, pre_grad)
@@ -528,18 +530,20 @@
         jnp.sum(gate_acc[...], axis=1, keepdims=True), (count, LANES)
     ).astype(bf16)
     first_level(last)
+    early = ne // 2
+    grads_in(last + 1, 1, early)
+    for k in range(1, early):
+        ret_copy(k).start()
+    grads_in(last + 1, early, ne)
+    for k in range(early, ne):
+        ret_copy(k).start()
+    plane_sum(last + 1)
     sum_level(last - 1, nz - 2)
     for level in range(1, nz - 1):
         sum_level(last, level)
-    for q in range(last - 1):
-        finish(q)
-    grads_in(last + 1)
-    for k in range(1, ne):
-        ret_copy(k).start()
-    plane_sum(last + 1)
     for turn in range(nz - 1):
         sum_turn(last + 1, turn)
-    for q in range(last - 1, last + 1):
+    for q in range(last + 1):
         finish(q)
     back[0:block, :] = ret[0:block, :]
 

time: 171 us -> 169 us (0.988)
  no operation moved by 1% of the time
where the time goes in v5:
time: 169 us
  Pallas kernels  163 us (96%)
  local copies, waits for them, and re-layouts  5.68 us (3%)
    pallas_call x1, Pallas kernels, fused(): pl.pallas_call(functools.partial(fused_kernel, nz, ne, block), out_shape=...  163 us
    unnamed x3, local copies, waits for them, and re-layouts  5.68 us

profile of v5, /device:TPU:0, one launch (start us, length us, event | category | flops | bytes accessed | tf_op | source)
XLA Modules:
  0.0 169.1 jit_solution(17422725497362796073)
XLA Ops:
  0.6 162.8 %shard_map.103 = (bf16[128,2048]{1,0:T(8,128)(2,1)}, bf16[2,128]{1,0:T(2,128)(2,1)}, f32[4,64,1536]{2,1,0:T(8,128)}) custom-call(bf16[128,2048]{1,0:T(8,128)(2,1)} %tok_ref.1, bf16[128,2048]{1,0:T(8,128)(2,1)} %dy_ref.1, s32[2,128]{1,0:T(2,128)} %bitcast.3, bf16[2,128]{1,0:T(2,128)(2,1)} %bitcast.4, bf16[1,512,1024]{2,1,0:T(8,128)(2,1)} %gu_ref.1, ...), custom_call_target="tpu_custom_call" | custom-call | flops 7247757312 | bytes 16777216 | tf_op jit(solution)/shard_map/pallas_call | solution.py:603
  163.4 1.9 %copy.14 = bf16[128,2048]{1,0:T(8,128)(2,1)} copy(bf16[128,2048]{1,0:T(8,128)(2,1)} %get-tuple-element.12) | data formatting | bytes 1048576
  165.3 1.1 copy.15
  166.4 2.7 %copy.16 = f32[4,64,1536]{2,1,0:T(8,128)} copy(f32[4,64,1536]{2,1,0:T(8,128)} %get-tuple-element.14) | data formatting | bytes 3145728

commit v6 on v5

--- a/solution.py
+++ b/solution.py
@@ -530,6 +530,8 @@
         jnp.sum(gate_acc[...], axis=1, keepdims=True), (count, LANES)
     ).astype(bf16)
     first_level(last)
+    for q in range(last - 1):
+        finish(q)
     early = ne // 2
     grads_in(last + 1, 1, early)
     for k in range(1, early):
@@ -543,7 +545,7 @@
         sum_level(last, level)
     for turn in range(nz - 1):
         sum_turn(last + 1, turn)
-    for q in range(last + 1):
+    for q in range(last - 1, last + 1):
         finish(q)
     back[0:block, :] = ret[0:block, :]
 

time: 169 us -> 169 us (level)
  no operation moved by 1% of the time
where the time goes in v6:
time: 169 us
  Pallas kernels  163 us (96%)
  local copies, waits for them, and re-layouts  5.68 us (3%)
    pallas_call x1, Pallas kernels, fused(): pl.pallas_call(functools.partial(fused_kernel, nz, ne, block), out_shape=...  163 us
    unnamed x3, local copies, waits for them, and re-layouts  5.68 us

profile of v6, /device:TPU:0, one launch (start us, length us, event | category | flops | bytes accessed | tf_op | source)
XLA Modules:
  0.0 169.1 jit_solution(17949067593934673809)
XLA Ops:
  0.6 162.8 %shard_map.103 = (bf16[128,2048]{1,0:T(8,128)(2,1)}, bf16[2,128]{1,0:T(2,128)(2,1)}, f32[4,64,1536]{2,1,0:T(8,128)}) custom-call(bf16[128,2048]{1,0:T(8,128)(2,1)} %tok_ref.1, bf16[128,2048]{1,0:T(8,128)(2,1)} %dy_ref.1, s32[2,128]{1,0:T(2,128)} %bitcast.3, bf16[2,128]{1,0:T(2,128)(2,1)} %bitcast.4, bf16[1,512,1024]{2,1,0:T(8,128)(2,1)} %gu_ref.1, ...), custom_call_target="tpu_custom_call" | custom-call | flops 7247757312 | bytes 16777216 | tf_op jit(solution)/shard_map/pallas_call | solution.py:605
  163.4 1.9 %copy.14 = bf16[128,2048]{1,0:T(8,128)(2,1)} copy(bf16[128,2048]{1,0:T(8,128)(2,1)} %get-tuple-element.12) | data formatting | bytes 1048576
  165.3 1.1 copy.15
  166.4 2.7 %copy.16 = f32[4,64,1536]{2,1,0:T(8,128)} copy(f32[4,64,1536]{2,1,0:T(8,128)} %get-tuple-element.14) | data formatting | bytes 3145728
